TPU v7x, 128 devices: a whole 4x4x4 slice. The times are simulated.
128 devices in a mesh: node: 8 (over y, core), local: 16 (over x, z).
Axes of the slice: x: 4, y: 4, z: 4, core: 2. Of those that a mesh axis runs over, the one named last changes fastest.
Arguments:
- tokens: bfloat16 [16384, 3584], P(('node', 'local')), may hold values from -6 to 6
- cotangent: bfloat16 [16384, 3584], P(('node', 'local')), may hold values from -6 to 6
- routes: int32 [16384, 2], P(('node', 'local')), may hold values from 0 to 31, as said below
- route_gates: float32 [16384, 2], P(('node', 'local')), may hold values from 0.2 to 1
- route_slots: int32 [16384, 2], P(('node', 'local')), may hold values from 0 to 8, as said below
- w_gate: bfloat16 [65536, 3584], P(('node', 'local')), may hold values from -0.09375 to 0.09375
- w_up: bfloat16 [65536, 3584], P(('node', 'local')), may hold values from -0.09375 to 0.09375
- w_down: bfloat16 [65536, 3584], P(('node', 'local')), may hold values from -0.125 to 0.125
Outputs:
- grad_tokens: bfloat16 [16384, 3584], P(('node', 'local'))
- grad_gate: bfloat16 [65536, 3584], P(('node', 'local'))
- grad_up: bfloat16 [65536, 3584], P(('node', 'local'))
- grad_down: bfloat16 [65536, 3584], P(('node', 'local'))
Inputs may be any that keep to these rules, and one draw needn't show every extreme that they name: `routes`: each row names 2 different experts, both of one group: g*4 to g*4 + 3 for one g. `route_slots`: among the routes of one device's tokens to one expert, those under 8 take distinct values; the value 8 marks a route dropped for lack of room.
All inputs are finite; a program needn't handle non-finite values.
Results may differ from a plain program's by a relative error of at most 0.0064.
Values may be sent and summed in bfloat16 or wider, within the bound.
A program may use at most 192 MiB of HBM per device.

v0:
```python
import jax
import jax.numpy as jnp
from jax import lax
from jax.sharding import PartitionSpec as P

EXP_NODE = 4


ROW_CONTRACT = (((1,), (1,)), ((), ()))
COL_CONTRACT = (((0,), (0,)), ((), ()))


def with_zero(values):
    return jnp.concatenate([values, jnp.zeros((1,) + values.shape[1:], values.dtype)], axis=0)


def expert_pass(expert_rows, expert_grads, gate_w, up_w, down_w):
    pre_gate = lax.dot_general(
        expert_rows, gate_w, ROW_CONTRACT, preferred_element_type=jnp.float32
    )
    pre_up = lax.dot_general(expert_rows, up_w, ROW_CONTRACT, preferred_element_type=jnp.float32)
    sigmoid_gate = jax.nn.sigmoid(pre_gate)
    active = pre_gate * sigmoid_gate
    hidden = (active * pre_up).astype(jnp.bfloat16)
    hidden_grad = lax.dot_general(
        expert_grads, down_w, ROW_CONTRACT, preferred_element_type=jnp.float32
    )
    gate_grad = (
        hidden_grad * pre_up * sigmoid_gate * (1.0 + pre_gate * (1.0 - sigmoid_gate))
    ).astype(jnp.bfloat16)
    up_grad = (hidden_grad * active).astype(jnp.bfloat16)
    down_wgrad = lax.dot_general(
        hidden, expert_grads, COL_CONTRACT, preferred_element_type=jnp.float32
    ).astype(jnp.bfloat16)
    gate_wgrad = lax.dot_general(
        gate_grad, expert_rows, COL_CONTRACT, preferred_element_type=jnp.float32
    ).astype(jnp.bfloat16)
    up_wgrad = lax.dot_general(
        up_grad, expert_rows, COL_CONTRACT, preferred_element_type=jnp.float32
    ).astype(jnp.bfloat16)
    row_partial = jnp.dot(gate_grad, gate_w, preferred_element_type=jnp.float32)
    row_partial = (row_partial + jnp.dot(up_grad, up_w, preferred_element_type=jnp.float32)).astype(
        jnp.bfloat16
    )
    return (row_partial, gate_wgrad, up_wgrad, down_wgrad)


def per_device(tokens, cotangent, routes, route_gates, route_slots, w_gate, w_up, w_down):
    tok_rows, model_width = tokens.shape
    top_count = routes.shape[1]
    node_count = lax.axis_size("node")
    local_count = lax.axis_size("local")
    device_count = node_count * local_count
    split_count = local_count // EXP_NODE
    expert_count = EXP_NODE * node_count
    capacity = tok_rows * top_count // expert_count
    kept_mask = route_slots < capacity
    gated = (route_gates[:, :, None] * cotangent[:, None, :].astype(jnp.float32)).astype(
        jnp.bfloat16
    )
    route_count = tok_rows * top_count
    route_ids = jnp.arange(route_count, dtype=jnp.int32)
    quarter = jnp.arange(split_count, dtype=jnp.int32)
    target = jnp.where(kept_mask, routes * capacity + route_slots, expert_count * capacity)
    slot_table = jnp.full((expert_count * capacity,), route_count, jnp.int32)
    slot_table = (
        slot_table.at[target.reshape(-1)]
        .set(route_ids, mode="drop")
        .reshape(expert_count, capacity)
    )
    peer_ids = jnp.arange(device_count, dtype=jnp.int32)
    peer_expert = peer_ids // local_count * EXP_NODE + peer_ids % local_count // split_count
    send_index = slot_table[peer_expert]
    send_rows = with_zero(tokens)[send_index // top_count]
    send_grads = with_zero(gated.reshape(route_count, model_width))[send_index]
    recv_rows, recv_grads = (
        lax.all_to_all(send_rows, ("node", "local"), split_axis=0, concat_axis=0, tiled=True),
        lax.all_to_all(send_grads, ("node", "local"), split_axis=0, concat_axis=0, tiled=True),
    )
    row_partial, gate_wgrad, up_wgrad, down_wgrad = expert_pass(
        recv_rows.reshape(-1, model_width),
        recv_grads.reshape(-1, model_width),
        w_gate,
        w_up,
        w_down,
    )
    returned = lax.all_to_all(
        row_partial.reshape(device_count, capacity, model_width),
        ("node", "local"),
        split_axis=0,
        concat_axis=0,
        tiled=True,
    )
    first_peer = routes // EXP_NODE * local_count + routes % EXP_NODE * split_count
    source_index = jnp.where(
        kept_mask[:, :, None],
        (first_peer[:, :, None] + quarter) * capacity + route_slots[:, :, None],
        device_count * capacity,
    )
    pieces = with_zero(returned.reshape(-1, model_width))[source_index]
    token_grad = jnp.sum(pieces.astype(jnp.float32), axis=(1, 2)).astype(jnp.bfloat16)
    return (token_grad, gate_wgrad, up_wgrad, down_wgrad)


def solution(mesh):
    return jax.shard_map(
        per_device,
        mesh=mesh,
        in_specs=(
            P(("node", "local"), None),
            P(("node", "local"), None),
            P(("node", "local"), None),
            P(("node", "local"), None),
            P(("node", "local"), None),
            P(("node", "local"), None),
            P(("node", "local"), None),
            P(("node", "local"), None),
        ),
        out_specs=(
            P(("node", "local"), None),
            P(("node", "local"), None),
            P(("node", "local"), None),
            P(("node", "local"), None),
        ),
        check_vma=False,
    )
```

profile of v0, /device:TPU:26, one launch (start us, length us, event | category | flops | bytes accessed | tf_op | source)
XLA Modules:
  0.0 374.0 jit_solution(11522190173175412529)
XLA Ops:
  0.7 0.7 fusion.28
  1.4 0.1 copy.16
  1.5 0.1 reshape.265
  1.6 1.4 scatter_custom_fusion
  3.1 0.1 reshape.266
  3.1 0.7 gather_fusion
  3.8 0.1 add_select_fusion.1
  3.8 0.1 reshape.289
  3.9 1.2 concatenate.10
  5.2 7.3 %gather_fusion.2 = bf16[1024,3584]{1,0:T(8,128)(2,1)} fusion(bf16[129,3584]{1,0:T(8,128)(2,1)S(1)} %concatenate.10, s32[1024]{0:T(1024)S(1)} %broadcast_clamp_fusion.1), kind=kCustom, calls=%fused_computation.2 | custom fusion | bytes 14684160 | tf_op jit(solution)/shard_map/gather | solution.py:74
  12.5 10.7 %all-to-all-start.1 = ((bf16[128,8,3584]{2,1,0:T(8,128)(2,1)}), bf16[128,8,3584]{2,1,0:T(8,128)(2,1)}, u32[]{:S(2)}, u32[]{:S(2)}) async-start(bf16[128,8,3584]{2,1,0:T(8,128)(2,1)} %bitcast.65), calls=%async_computation.1 | async-start | bytes 14680064 | tf_op jit(solution)/shard_map/all_to_all | solution.py:77
  23.2 0.0 copy-done.2
  23.2 0.1 copy.15
  23.3 0.1 mul.76
  23.4 0.1 reshape.281
  23.5 0.0 copy-done
  23.5 2.8 mul.78
  26.3 5.6 %mul.79 = f32[256,3584]{1,0:T(8,128)} reshape(f32[128,2,3584]{2,1,0:T(2,128)} %mul.78) | data formatting | bytes 7340032 | tf_op jit(solution)/shard_map/mul | solution.py:58
  31.9 2.4 multiply_convert_fusion
  34.3 0.1 concatenate.9
  34.5 7.3 %gather_fusion.1 = bf16[1024,3584]{1,0:T(8,128)(2,1)} fusion(bf16[257,3584]{1,0:T(8,128)(2,1)S(1)} %concatenate.9, s32[1024]{0:T(1024)S(1)} %broadcast_clamp_fusion.2), kind=kCustom, calls=%fused_computation.1 | custom fusion | bytes 14684160 | tf_op jit(solution)/shard_map/gather | solution.py:75
  41.8 67.0 %all-to-all-done.1 = bf16[128,8,3584]{2,1,0:T(8,128)(2,1)} async-done(((bf16[128,8,3584]{2,1,0:T(8,128)(2,1)}), bf16[128,8,3584]{2,1,0:T(8,128)(2,1)}, u32[]{:S(2)}, u32[]{:S(2)}) %all-to-all-start.1) | async-done | bytes 7340064 | tf_op jit(solution)/shard_map/all_to_all | solution.py:77
  108.8 10.2 %all-to-all-start = ((bf16[128,8,3584]{2,1,0:T(8,128)(2,1)}), bf16[128,8,3584]{2,1,0:T(8,128)(2,1)}, u32[]{:S(2)}, u32[]{:S(2)}) async-start(bf16[128,8,3584]{2,1,0:T(8,128)(2,1)} %bitcast.66), calls=%async_computation | async-start | bytes 14680064 | tf_op jit(solution)/shard_map/all_to_all | solution.py:78
  119.0 0.0 copy-start.4
  119.0 9.6 %fusion.4 = f32[1024,512]{1,0:T(8,128)} fusion(bf16[512,3584]{1,0:T(8,128)(2,1)} %param.13, bf16[128,8,3584]{2,1,0:T(8,128)(2,1)} %all-to-all-done.1), kind=kOutput, calls=%fused_computation.10 | convolution fusion | flops 3758096384 | bytes 13107200 | tf_op jit(solution)/shard_map/dot_general | solution.py:18
  128.6 0.0 copy-done.4
  128.6 7.6 %fusion.6 = f32[1024,512]{1,0:T(8,128)} fusion(bf16[512,3584]{1,0:T(8,128)(2,1)S(1)} %copy-done.4, bf16[128,8,3584]{2,1,0:T(8,128)(2,1)} %all-to-all-done.1), kind=kOutput, calls=%fused_computation.12 | convolution fusion | flops 3758096384 | bytes 13107200 | tf_op jit(solution)/shard_map/dot_general | solution.py:21
  136.2 68.5 %all-to-all-done = bf16[128,8,3584]{2,1,0:T(8,128)(2,1)} async-done(((bf16[128,8,3584]{2,1,0:T(8,128)(2,1)}), bf16[128,8,3584]{2,1,0:T(8,128)(2,1)}, u32[]{:S(2)}, u32[]{:S(2)}) %all-to-all-start) | async-done | bytes 7340064 | tf_op jit(solution)/shard_map/all_to_all | solution.py:78
  204.6 10.1 %multiply_convert_fusion.2 = (bf16[1024,512]{1,0:T(8,128)(2,1)S(1)}, bf16[1024,512]{1,0:T(8,128)(2,1)S(1)}) fusion(f32[1024,512]{1,0:T(8,128)} %fusion.4, f32[1024,512]{1,0:T(8,128)} %fusion.6, bf16[512,3584]{1,0:T(8,128)(2,1)} %param.15, bf16[128,8,3584]{2,1,0:T(8,128)(2,1)} %all-to-all-done), kind=kOutput, calls=%fused_computation.24 | convolution fusion | flops 3764912128 | bytes 17301504 | tf_op jit(solution)/shard_map/dot_general | solution.py:25
  214.7 0.0 copy-done.3
  214.7 0.0 copy-start.5
  214.8 7.3 %fusion.35 = f32[1024,3584]{1,0:T(8,128)} fusion(bf16[1024,512]{1,0:T(8,128)(2,1)S(1)} %get-tuple-element.5, bf16[512,3584]{1,0:T(8,128)(2,1)S(1)} %copy-done.3), kind=kOutput, calls=%fused_computation.70 | convolution fusion | flops 3758096384 | bytes 19398656 | tf_op jit(solution)/shard_map/dot_general | solution.py:41
  222.1 0.0 copy-done.5
  222.1 9.3 %fusion.12 = bf16[128,8,3584]{2,1,0:T(8,128)(2,1)} fusion(f32[1024,3584]{1,0:T(8,128)} %fusion.35, bf16[1024,512]{1,0:T(8,128)(2,1)S(1)} %get-tuple-element.4, bf16[512,3584]{1,0:T(8,128)(2,1)S(1)} %copy-done.5), kind=kOutput, calls=%fused_computation.18 | convolution fusion | flops 3765436416 | bytes 26738688 | tf_op jit(solution)/shard_map/dot_general | solution.py:42
  231.3 10.2 %all-to-all-start.2 = ((bf16[128,8,3584]{2,1,0:T(8,128)(2,1)}), bf16[128,8,3584]{2,1,0:T(8,128)(2,1)}, u32[]{:S(2)}, u32[]{:S(2)}) async-start(bf16[128,8,3584]{2,1,0:T(8,128)(2,1)} %fusion.12), calls=%async_computation.2 | async-start | bytes 14680064 | tf_op jit(solution)/shard_map/all_to_all | solution.py:87
  241.5 0.1 copy.19
  241.6 0.1 copy.17
  241.8 0.1 copy.18
  241.9 0.6 compare_select_fusion
  242.5 0.2 reshape.297
  242.7 8.5 %fusion.19 = bf16[512,3584]{1,0:T(8,128)(2,1)} fusion(bf16[1024,512]{1,0:T(8,128)(2,1)S(1)} %get-tuple-element.4, bf16[128,8,3584]{2,1,0:T(8,128)(2,1)} %all-to-all-done.1), kind=kOutput, calls=%fused_computation.21 | convolution fusion | flops 3759931392 | bytes 12058624 | tf_op jit(solution)/shard_map/dot_general | solution.py:38
  251.2 8.7 %fusion.16 = bf16[512,3584]{1,0:T(8,128)(2,1)} fusion(bf16[1024,512]{1,0:T(8,128)(2,1)S(1)} %get-tuple-element.5, bf16[128,8,3584]{2,1,0:T(8,128)(2,1)} %all-to-all-done.1), kind=kOutput, calls=%fused_computation.20 | convolution fusion | flops 3759931392 | bytes 12058624 | tf_op jit(solution)/shard_map/dot_general | solution.py:35
  259.9 8.8 %fusion.13 = bf16[512,3584]{1,0:T(8,128)(2,1)} fusion(bf16[128,8,3584]{2,1,0:T(8,128)(2,1)} %all-to-all-done, f32[1024,512]{1,0:T(8,128)S(1)} %copy-done.7, f32[1024,512]{1,0:T(8,128)S(1)} %copy-done.6), kind=kOutput, calls=%fused_computation.19 | convolution fusion | flops 3763077120 | bytes 15204352 | tf_op jit(solution)/shard_map/dot_general | solution.py:32
  268.7 58.5 %all-to-all-done.2 = bf16[128,8,3584]{2,1,0:T(8,128)(2,1)} async-done(((bf16[128,8,3584]{2,1,0:T(8,128)(2,1)}), bf16[128,8,3584]{2,1,0:T(8,128)(2,1)}, u32[]{:S(2)}, u32[]{:S(2)}) %all-to-all-start.2) | async-done | bytes 7340064 | tf_op jit(solution)/shard_map/all_to_all | solution.py:87
  327.1 6.5 %concatenate.11 = bf16[1025,3584]{1,0:T(8,128)(2,1)} pad(bf16[1024,3584]{1,0:T(8,128)(2,1)} %bitcast.8, bf16[]{:T(256)} %constant.85.clone.1), padding=0_1x0_0 | pad | bytes 14687234 | tf_op jit(solution)/shard_map/concatenate | solution.py:14
  333.7 17.8 %gather_fusion.3 = bf16[1024,3584]{1,0:T(8,128)(2,1)} fusion(bf16[1025,3584]{1,0:T(8,128)(2,1)} %concatenate.11, s32[1024]{0:T(1024)S(1)} %broadcast_clamp_fusion), kind=kCustom, calls=%fused_computation.3 | custom fusion | bytes 14684160 | tf_op jit(solution)/shard_map/gather | solution.py:100
  351.5 12.6 %reshape.300 = bf16[128,2,4,3584]{3,2,1,0:T(4,128)(2,1)} reshape(bf16[1024,3584]{1,0:T(8,128)(2,1)} %gather_fusion.3) | data formatting | bytes 14680064 | tf_op jit(solution)/shard_map/gather | solution.py:100
  364.1 9.9 %reduce_sum.12 = bf16[128,3584]{1,0:T(8,128)(2,1)} reduce(bf16[128,2,4,3584]{3,2,1,0:T(4,128)(2,1)} %reshape.300, bf16[]{:T(256)} %constant.85.clone.1), dimensions={1,2}, to_apply=%region_1.2 | reduce | flops 3211264 | bytes 8257538 | tf_op jit(solution)/shard_map/reduce_sum | solution.py:101
  (17 shorter events, 0.1 us)
Async XLA Ops:
  12.5 10.7 %copy-start.2 = (f32[128,2]{0,1:T(2,128)S(1)}, f32[128,2]{0,1:T(2,128)}, u32[]{:S(2)}) copy-start(f32[128,2]{0,1:T(2,128)} %param.11) | copy-start | bytes 3076
  12.5 11.0 %copy-start = (bf16[128,3584]{1,0:T(8,128)(2,1)S(1)}, bf16[128,3584]{1,0:T(8,128)(2,1)}, u32[]{:S(2)}) copy-start(bf16[128,3584]{1,0:T(8,128)(2,1)} %param.9) | copy-start | bytes 2752516
  12.5 96.3 %all-to-all-start.1 = ((bf16[128,8,3584]{2,1,0:T(8,128)(2,1)}), bf16[128,8,3584]{2,1,0:T(8,128)(2,1)}, u32[]{:S(2)}, u32[]{:S(2)}) async-start(bf16[128,8,3584]{2,1,0:T(8,128)(2,1)} %bitcast.65), calls=%async_computation.1 | async-start | bytes 14680064 | tf_op jit(solution)/shard_map/all_to_all | solution.py:77
  108.8 95.8 %all-to-all-start = ((bf16[128,8,3584]{2,1,0:T(8,128)(2,1)}), bf16[128,8,3584]{2,1,0:T(8,128)(2,1)}, u32[]{:S(2)}, u32[]{:S(2)}) async-start(bf16[128,8,3584]{2,1,0:T(8,128)(2,1)} %bitcast.66), calls=%async_computation | async-start | bytes 14680064 | tf_op jit(solution)/shard_map/all_to_all | solution.py:78
  119.0 9.6 %copy-start.4 = (bf16[512,3584]{1,0:T(8,128)(2,1)S(1)}, bf16[512,3584]{1,0:T(8,128)(2,1)}, u32[]{:S(2)}) copy-start(bf16[512,3584]{1,0:T(8,128)(2,1)} %param.14) | copy-start | bytes 11010052
  204.6 10.1 %copy-start.3 = (bf16[512,3584]{1,0:T(8,128)(2,1)S(1)}, bf16[512,3584]{1,0:T(8,128)(2,1)}, u32[]{:S(2)}) copy-start(bf16[512,3584]{1,0:T(8,128)(2,1)} %param.13) | copy-start | bytes 11010052
  214.7 7.3 %copy-start.5 = (bf16[512,3584]{1,0:T(8,128)(2,1)S(1)}, bf16[512,3584]{1,0:T(8,128)(2,1)}, u32[]{:S(2)}) copy-start(bf16[512,3584]{1,0:T(8,128)(2,1)} %param.14) | copy-start | bytes 11010052
  231.3 10.2 %copy-start.1 = (s32[128,2]{0,1:T(2,128)S(1)}, s32[128,2]{0,1:T(2,128)}, u32[]{:S(2)}) copy-start(s32[128,2]{0,1:T(2,128)} %param.12) | copy-start | bytes 3076
  231.3 95.8 %all-to-all-start.2 = ((bf16[128,8,3584]{2,1,0:T(8,128)(2,1)}), bf16[128,8,3584]{2,1,0:T(8,128)(2,1)}, u32[]{:S(2)}, u32[]{:S(2)}) async-start(bf16[128,8,3584]{2,1,0:T(8,128)(2,1)} %fusion.12), calls=%async_computation.2 | async-start | bytes 14680064 | tf_op jit(solution)/shard_map/all_to_all | solution.py:87
  251.2 8.7 %copy-start.6 = (f32[1024,512]{1,0:T(8,128)S(1)}, f32[1024,512]{1,0:T(8,128)}, u32[]{:S(2)}) copy-start(f32[1024,512]{1,0:T(8,128)} %fusion.4) | copy-start | bytes 6291460
  251.2 8.7 %copy-start.7 = (f32[1024,512]{1,0:T(8,128)S(1)}, f32[1024,512]{1,0:T(8,128)}, u32[]{:S(2)}) copy-start(f32[1024,512]{1,0:T(8,128)} %fusion.6) | copy-start | bytes 6291460
where the time goes:
time: 380 us; the launch traced here: 374 us
  waiting for transfers between devices  194 us (51%)
  matrix products  69.9 us (18%)
  local copies, waits for them, and re-layouts  64.7 us (17%)
  starting transfers between devices  31 us (8%)
  other arithmetic  13.7 us (4%)
    all_to_all x1, waiting for transfers between devices, per_device(): lax.all_to_all(send_grads, ('node', 'local'), split_axis=0, concat_axis=0...  68.5 us
    all_to_all x1, waiting for transfers between devices, per_device(): lax.all_to_all(send_rows, ('node', 'local'), split_axis=0, concat_axis=0,...  67 us
    all_to_all x1, waiting for transfers between devices, per_device(): lax.all_to_all(row_partial.reshape(device_count, capacity, model_width),...  58.5 us
    gather x2, local copies, waits for them, and re-layouts, per_device(): pieces = with_zero(returned.reshape(-1, model_width))[source_index]  30.4 us
    all_to_all x1, starting transfers between devices, per_device(): lax.all_to_all(send_rows, ('node', 'local'), split_axis=0, concat_axis=0,...  10.7 us
    all_to_all x1, starting transfers between devices, per_device(): lax.all_to_all(row_partial.reshape(device_count, capacity, model_width),...  10.2 us
    all_to_all x1, starting transfers between devices, per_device(): lax.all_to_all(send_grads, ('node', 'local'), split_axis=0, concat_axis=0...  10.2 us
    dot_general x1, matrix products, expert_pass(): lax.dot_general(expert_grads, down_w, ROW_CONTRACT, preferred_element_typ...  10.1 us
  transfers between devices with their start and end apart: 3, of which 3 were waited for; matrix products, arithmetic and copies ran while one was open for 17% of the time, Pallas kernels for 0%

commit v1 on v0

v1 whole, which is shorter than its diff:
```python
import jax
import jax.numpy as jnp
from jax import lax
from jax.experimental import pallas as pl
from jax.experimental.pallas import tpu as pltpu
from jax.sharding import PartitionSpec as P

MESH = pl.DeviceIdType.MESH
BF16, F32 = jnp.bfloat16, jnp.float32
CAP = 8
TOK = 128
D = 3584
HDEV = 512
ROWS = 256
BLK = 16
TILE = 512
TILES = D // TILE
NT = (((1,), (1,)), ((), ()))
NN = (((1,), (0,)), ((), ()))


def mm(a, b, dims=NN):
    return lax.dot_general(a, b, dims, preferred_element_type=F32)


def mod4(v):
    return lax.rem(v, 4)


def kernel(
    tok, cot, routes, slots, gates, wg_h, wu_h, wd_h,
    out_tok, og_h, ou_h, od_h,
    wg, wu, wd, xs, gs, snd, tok_o, cot_o, meta, onehot, ret,
    swap_snd, swap_rcv, sum_snd, sum_rcv, ht, ggt, ugt, gg, ug, stage,
    w_sem, cx_send, cx_recv, m_send, m_recv, own_sem, d_send, d_recv,
    z_send, z_recv, f_send, r_send, r_recv, rown_sem,
    t_send, t_recv, o_send, o_recv, st_sem,
):
    node, local = lax.axis_index("node"), lax.axis_index("local")
    y, c = lax.div(node, 2), lax.rem(node, 2)
    x, z = lax.div(local, 4), lax.rem(local, 4)

    def dev(dx, dy, dz, flip=False):
        core = 1 - c if flip else c
        return (mod4(y + dy) * 2 + core, mod4(x + dx) * 4 + mod4(z + dz))

    def remote(src, dst, ssem, rsem, target):
        return pltpu.make_async_remote_copy(
            src_ref=src, dst_ref=dst, send_sem=ssem, recv_sem=rsem,
            device_id=target, device_id_type=MESH,
        )

    here = dev(0, 0, 0, True)

    def wait_recv(ref, sem):
        remote(ref, ref, sem, sem, here).wait_recv()

    def wait_send(ref, sem):
        remote(ref, ref, sem, sem, here).wait_send()

    loads = [
        pltpu.make_async_copy(src, dst, w_sem.at[k])
        for k, (src, dst) in enumerate(((wg_h, wg), (wu_h, wu), (wd_h, wd)))
    ]
    for load in loads:
        load.start()

    barrier = pltpu.get_barrier_semaphore()

    def greet(k, carry):
        pl.semaphore_signal(
            barrier, inc=1, device_id=dev(lax.rem(k, 4), lax.div(k, 4), 0), device_id_type=MESH
        )
        return carry

    lax.fori_loop(1, 16, greet, 0)
    for dz in (1, 2, 3):
        pl.semaphore_signal(barrier, inc=1, device_id=dev(0, 0, dz), device_id_type=MESH)
    pl.semaphore_signal(barrier, inc=1, device_id=here, device_id_type=MESH)

    lane = lax.broadcasted_iota(jnp.int32, (TOK, 128), 1)
    target = jnp.where(slots[...] < CAP, routes[...] * CAP + slots[...], -1).astype(F32)
    gate = gates[...]
    meta[0, 0] = jnp.where(
        lane == 0, target[:, 0:1],
        jnp.where(lane == 1, target[:, 1:2], jnp.where(lane == 2, gate[:, 0:1], gate[:, 1:2])),
    )
    pl.semaphore_wait(barrier, 19)

    swaps = [
        remote(src, dst, cx_send.at[k], cx_recv.at[k], here)
        for k, (src, dst) in enumerate(
            ((meta.at[0, 0], meta.at[0, 1]), (tok, tok_o), (cot, cot_o))
        )
    ]
    for swap in swaps:
        swap.start()

    def row_target(r, core):
        e = (mod4(y + (r >> 6)) * 2 + c) * 4 + mod4(x + ((r >> 4) & 3))
        return jnp.where(((r >> 3) & 1) == core, e * CAP + (r & 7), -2).astype(F32)

    swaps[0].wait_recv()
    metas = [
        remote(meta.at[0], meta.at[4 - dz], m_send.at[dz - 1], m_recv.at[3 - dz], dev(0, 0, dz))
        for dz in (1, 2, 3)
    ]
    for m in metas:
        m.start()

    row_ids = lax.broadcasted_iota(jnp.int32, (ROWS, TOK), 0)
    row_gate = jnp.zeros((ROWS, 1), F32)
    for k, core in enumerate((c, 1 - c)):
        want = row_target(row_ids, core)
        mt = meta[0, k].T
        hit0, hit1 = want == mt[0:1, :], want == mt[1:2, :]
        onehot[k] = (jnp.where(hit0, 1.0, 0.0) + jnp.where(hit1, 1.0, 0.0)).astype(BF16)
        picked = jnp.where(hit0, mt[2:3, :], 0.0) + jnp.where(hit1, mt[3:4, :], 0.0)
        row_gate = row_gate + jnp.sum(picked, axis=1, keepdims=True)

    own_rows = pl.ds(pl.multiple_of((y * 4 + x) * BLK, BLK), BLK)

    def dispatch(a, buf):
        pltpu.make_async_copy(snd.at[a, pl.ds(0, BLK)], buf.at[own_rows], own_sem.at[a]).start()

        def send(k, carry):
            i, j = lax.div(k, 4), lax.rem(k, 4)
            remote(
                snd.at[a, pl.ds(pl.multiple_of(k * BLK, BLK), BLK)], buf.at[own_rows],
                d_send.at[a], d_recv.at[a, i], dev(j, i, 0),
            ).start()
            return carry

        lax.fori_loop(1, 16, send, 0)

    def tiled(body):
        def step(t, carry):
            body(pl.ds(pl.multiple_of(t * TILE, TILE), TILE))
            return carry

        lax.fori_loop(0, TILES, step, 0)

    swaps[1].wait_recv()

    def build_x(cols):
        rows = mm(onehot[0], tok[:, cols]) + mm(onehot[1], tok_o[:, cols])
        snd[0, :, cols] = rows.astype(BF16)

    tiled(build_x)
    dispatch(0, xs)
    swaps[2].wait_recv()

    def build_g(cols):
        rows = mm(onehot[0], cot[:, cols]) + mm(onehot[1], cot_o[:, cols])
        snd[1, :, cols] = (row_gate * rows).astype(BF16)

    tiled(build_g)
    dispatch(1, gs)

    def group(i):
        return pl.multiple_of(mod4(y + 4 - i) * 64, 64)

    bufs = (xs, gs)
    for i in range(4):
        off = group(i)
        for a, buf in enumerate(bufs):
            if i == 0:
                pltpu.make_async_copy(
                    snd.at[a, pl.ds(0, BLK)], buf.at[own_rows], own_sem.at[a]
                ).wait()
            wait_recv(buf.at[pl.ds(0, 48 if i == 0 else 64)], d_recv.at[a, i])
            for k, (dz, slot) in enumerate(((1, 3), (3, 1))):
                remote(
                    buf.at[pl.ds(off, 64)], buf.at[pl.ds(off + slot * ROWS, 64)],
                    z_send.at[k, a, i], z_recv.at[slot - 1, a, i], dev(0, 0, dz),
                ).start()

    def wait_z(slot, a, i):
        wait_recv(bufs[a].at[pl.ds(0, 64)], z_recv.at[slot - 1, a, i])

    def forward(i):
        off = group(i)
        for a, slot, dz in ((0, 3, 1), (1, 1, 3)):
            wait_z(slot, a, i)
            remote(
                bufs[a].at[pl.ds(off + slot * ROWS, 64)], bufs[a].at[pl.ds(off + 2 * ROWS, 64)],
                f_send.at[a, i], z_recv.at[1, a, i], dev(0, 0, dz),
            ).start()

    def expert_pass(d, slot):
        rows = pl.ds(d * ROWS, ROWS)

        def hidden_part(h, carry):
            hid = pl.ds(pl.multiple_of(h * 256, 256), 256)
            pre_gate = mm(wg[hid, :], xs[rows, :], NT)
            pre_up = mm(wu[hid, :], xs[rows, :], NT)
            hidden_grad = mm(wd[hid, :], gs[rows, :], NT)
            sig = jax.nn.sigmoid(pre_gate)
            active = pre_gate * sig
            ht[hid, rows] = (active * pre_up).astype(BF16)
            gate_grad = hidden_grad * pre_up * sig * (1.0 + pre_gate * (1.0 - sig))
            up_grad = hidden_grad * active
            ggt[hid, rows] = gate_grad.astype(BF16)
            ugt[hid, rows] = up_grad.astype(BF16)
            gg[:, hid] = gate_grad.T.astype(BF16)
            ug[:, hid] = up_grad.T.astype(BF16)
            return carry

        lax.fori_loop(0, HDEV // 256, hidden_part, 0)

        def part(cols):
            snd[slot, :, cols] = (mm(gg[...], wg[:, cols]) + mm(ug[...], wu[:, cols])).astype(BF16)

        tiled(part)
        own = pltpu.make_async_copy(
            snd.at[slot, own_rows], ret.at[pl.ds(d * ROWS, BLK)], rown_sem.at[d]
        )
        own.start()

        def send(k, carry):
            i, j = lax.div(k, 4), lax.rem(k, 4)
            row = pl.multiple_of((mod4(y + 4 - i) * 4 + mod4(x + 4 - j)) * BLK, BLK)
            remote(
                snd.at[slot, pl.ds(row, BLK)],
                ret.at[pl.ds(pl.multiple_of(d * ROWS + k * BLK, BLK), BLK)],
                r_send.at[d], r_recv.at[d], dev(4 - j, 4 - i, 0),
            ).start()
            return carry

        lax.fori_loop(1, 16, send, 0)
        own.wait()

    def returned(d, slot):
        wait_send(snd.at[slot, pl.ds(0, 240)], r_send.at[d])

    def swap_copy(d):
        return remote(swap_snd.at[d], swap_rcv.at[d], t_send.at[d], t_recv.at[d], here)

    def sum_copy(d):
        return remote(
            sum_snd.at[d], sum_rcv.at[3 - d], o_send.at[d - 1], o_recv.at[3 - d], dev(0, 0, d)
        )

    def combine(d):
        wait_recv(ret.at[pl.ds(d * ROWS, 240)], r_recv.at[d])
        if d:
            wait_recv(meta.at[d], m_recv.at[d - 1])
        col_ids = lax.broadcasted_iota(jnp.int32, (TOK, ROWS), 1)
        picks = []
        for k, core in enumerate((c, 1 - c)):
            want = row_target(col_ids, core)
            m = meta[d, k]
            pick = jnp.where(want == m[:, 0:1], 1.0, 0.0) + jnp.where(want == m[:, 1:2], 1.0, 0.0)
            picks.append(pick.astype(BF16))

        def sums(cols):
            rows = ret[pl.ds(d * ROWS, ROWS), cols]
            sum_snd[d, :, cols] = mm(picks[0], rows).astype(BF16)
            swap_snd[d, :, cols] = mm(picks[1], rows).astype(BF16)

        tiled(sums)
        swap_copy(d).start()

    def pass_on(d):
        swap_copy(d).wait_recv()

        def add(cols):
            both = sum_snd[d, :, cols].astype(F32) + swap_rcv[d, :, cols].astype(F32)
            sum_snd[d, :, cols] = both.astype(BF16)

        tiled(add)
        if d:
            sum_copy(d).start()

    forward(0)
    for load in loads:
        load.wait()
    for a in range(2):
        wait_send(snd.at[a, pl.ds(0, 240)], d_send.at[a])
    expert_pass(0, 0)
    for i in range(1, 4):
        forward(i)
    for i in range(4):
        wait_z(3, 1, i)
    expert_pass(3, 1)
    for i in range(4):
        wait_z(1, 0, i)
    returned(0, 0)
    expert_pass(1, 0)
    combine(0)
    pass_on(0)
    for i in range(4):
        for a in range(2):
            wait_z(2, a, i)
    returned(3, 1)
    expert_pass(2, 1)
    combine(3)
    combine(1)
    pass_on(3)
    pass_on(1)

    jobs = ((ggt, xs, og_h), (ugt, xs, ou_h), (ht, gs, od_h))

    def stage_copy(t, n, slot):
        cols = pl.ds(pl.multiple_of(t * TILE, TILE), TILE)
        return pltpu.make_async_copy(stage.at[slot, n], jobs[n][2].at[:, cols], st_sem.at[slot, n])

    def wgrad(t, carry):
        slot = lax.rem(t, 2)
        cols = pl.ds(pl.multiple_of(t * TILE, TILE), TILE)
        for n, (left, right, _) in enumerate(jobs):

            @pl.when(t >= 2)
            def _():
                stage_copy(t - 2, n, slot).wait()

            stage[slot, n] = mm(left[...], right[:, cols]).astype(BF16)
            stage_copy(t, n, slot).start()
        return carry

    lax.fori_loop(0, TILES, wgrad, 0)

    combine(2)
    pass_on(2)
    for d in (3, 1, 2):
        wait_recv(sum_rcv.at[d - 1], o_recv.at[d - 1])

    def total(cols):
        acc = sum_snd[0, :, cols].astype(F32)
        for k in range(3):
            acc = acc + sum_rcv[k, :, cols].astype(F32)
        out_tok[:, cols] = acc.astype(BF16)

    tiled(total)

    for t in (TILES - 2, TILES - 1):
        for n in range(3):
            stage_copy(t, n, t % 2).wait()
    for swap in swaps:
        swap.wait_send()
    for m in metas:
        m.wait_send()
    for i in range(4):
        for a, buf in enumerate(bufs):
            for k in range(2):
                wait_send(buf.at[pl.ds(0, 64)], z_send.at[k, a, i])
            wait_send(buf.at[pl.ds(0, 64)], f_send.at[a, i])
    returned(1, 0)
    returned(2, 1)
    for d in range(4):
        swap_copy(d).wait_send()
        if d:
            sum_copy(d).wait_send()


def per_device(tokens, cotangent, routes, route_gates, route_slots, w_gate, w_up, w_down):
    vmem, hbm = pl.BlockSpec(memory_space=pltpu.VMEM), pl.BlockSpec(memory_space=pl.ANY)
    dma = pltpu.SemaphoreType.DMA
    grad = jax.ShapeDtypeStruct((HDEV, D), BF16)
    return pl.pallas_call(
        kernel,
        out_shape=(jax.ShapeDtypeStruct((TOK, D), BF16), grad, grad, grad),
        in_specs=[vmem] * 5 + [hbm] * 3,
        out_specs=(vmem, hbm, hbm, hbm),
        scratch_shapes=[
            pltpu.VMEM((HDEV, D), BF16),
            pltpu.VMEM((HDEV, D), BF16),
            pltpu.VMEM((HDEV, D), BF16),
            pltpu.VMEM((4 * ROWS, D), BF16),
            pltpu.VMEM((4 * ROWS, D), BF16),
            pltpu.VMEM((2, ROWS, D), BF16),
            pltpu.VMEM((TOK, D), BF16),
            pltpu.VMEM((TOK, D), BF16),
            pltpu.VMEM((4, 2, TOK, 128), F32),
            pltpu.VMEM((2, ROWS, TOK), BF16),
            pltpu.VMEM((4 * ROWS, D), BF16),
            pltpu.VMEM((4, TOK, D), BF16),
            pltpu.VMEM((4, TOK, D), BF16),
            pltpu.VMEM((4, TOK, D), BF16),
            pltpu.VMEM((3, TOK, D), BF16),
            pltpu.VMEM((HDEV, 4 * ROWS), BF16),
            pltpu.VMEM((HDEV, 4 * ROWS), BF16),
            pltpu.VMEM((HDEV, 4 * ROWS), BF16),
            pltpu.VMEM((ROWS, HDEV), BF16),
            pltpu.VMEM((ROWS, HDEV), BF16),
            pltpu.VMEM((2, 3, HDEV, TILE), BF16),
            dma((3,)), dma((3,)), dma((3,)), dma((3,)), dma((3,)),
            dma((2,)), dma((2,)), dma((2, 4)),
            dma((2, 2, 4)), dma((3, 2, 4)), dma((2, 4)),
            dma((4,)), dma((4,)), dma((4,)),
            dma((4,)), dma((4,)), dma((3,)), dma((3,)), dma((2, 3)),
        ],
        compiler_params=pltpu.CompilerParams(
            collective_id=0, has_side_effects=True, vmem_limit_bytes=63 * 2**20
        ),
        cost_estimate=pl.CostEstimate(
            flops=8 * 2 * 1024 * D * HDEV, bytes_accessed=6 * 2 * HDEV * D, transcendentals=1024 * HDEV
        ),
    )(tokens, cotangent, routes, route_slots, route_gates, w_gate, w_up, w_down)


def solution(mesh):
    spec = P(("node", "local"), None)
    return jax.shard_map(
        per_device, mesh=mesh, in_specs=(spec,) * 8, out_specs=(spec,) * 4, check_vma=False
    )
```

time: 380 us -> 244 us (0.64)
  Pallas kernels: 0 us -> 225 us
  waiting for transfers between devices: 194 us -> 0 us
  matrix products: 69.9 us -> 0 us
  local copies, waits for them, and re-layouts: 64.7 us -> 15.9 us
  starting transfers between devices: 31 us -> 0 us
  other arithmetic: 13.7 us -> 0 us
    pallas_call x0 -> x1, Pallas kernels: none -> 225 us  [per_device(): pl.pallas_call(kernel, out_shape=(jax.ShapeDtypeStruct((TOK, D), BF16), g...]
    all_to_all x3 -> x0, waiting for transfers between devices: 194 us -> none  [the longest x1 68.5 us: per_device(): lax.all_to_all(send_grads, ('node', 'local'), split_axis=0, concat_axis=0...]
    dot_general x8 -> x0, matrix products: 69.9 us -> none  [the longest x1 10.1 us: expert_pass(): lax.dot_general(expert_grads, down_w, ROW_CONTRACT, preferred_element_typ...]
    gather x5 -> x0, local copies, waits for them, and re-layouts: 45.7 us -> none  [the longest x2 30.4 us: per_device(): pieces = with_zero(returned.reshape(-1, model_width))[source_index]]
    all_to_all x3 -> x0, starting transfers between devices: 31 us -> none  [the longest x1 10.7 us: per_device(): lax.all_to_all(send_rows, ('node', 'local'), split_axis=0, concat_axis=0,...]
    unnamed x18 -> x11, local copies, waits for them, and re-layouts: 0.26 us -> 15.9 us
    reduce_sum x1 -> x0, other arithmetic: 9.93 us -> none  [per_device(): jnp.sum(pieces.astype(jnp.float32), axis=(1, 2)).astype(jnp.bfloat16)]
    mul x3 -> x0, local copies, waits for them, and re-layouts: 8.53 us -> none  [per_device(): route_gates[:, :, None] * cotangent[:, None, :].astype(jnp.float32)]
  transfers between devices with their start and end apart: 3 -> 0, of which waited for: 3 -> 0; matrix products, arithmetic and copies ran while one was open for 17% -> 0% of each run, Pallas kernels for 0% -> 0%
where the time goes in v1:
time: 244 us; the launch traced here: 241 us
  Pallas kernels  225 us (92%)
  local copies, waits for them, and re-layouts  15.9 us (7%)
    pallas_call x1, Pallas kernels, per_device(): pl.pallas_call(kernel, out_shape=(jax.ShapeDtypeStruct((TOK, D), BF16), g...  225 us
    unnamed x11, local copies, waits for them, and re-layouts  15.9 us

profile of v1, /device:TPU:26, one launch (start us, length us, event | category | flops | bytes accessed | tf_op | source)
XLA Modules:
  0.0 241.4 jit_solution(4585158768685639569)
XLA Ops:
  0.6 1.4 copy.12.routes
  2.0 1.4 copy.14.gates
  3.5 1.4 copy.13.slots
  4.9 224.9 %shard_map.111 = (bf16[128,3584]{1,0:T(8,128)(2,1)}, bf16[512,3584]{1,0:T(8,128)(2,1)}, bf16[512,3584]{1,0:T(8,128)(2,1)}, bf16[512,3584]{1,0:T(8,128)(2,1)}) custom-call(bf16[128,3584]{1,0:T(8,128)(2,1)} %tok.1, bf16[128,3584]{1,0:T(8,128)(2,1)} %cot.1, s32[128,2]{1,0:T(8,128)} %copy.12.routes, s32[128,2]{1,0:T(8,128)} %copy.13.slots, ...), custom_call_target="tpu_custom_call" | custom-call | flops 30064771072 | bytes 22020096 | tf_op jit(solution)/shard_map/pallas_call | solution.py:360
  229.8 2.2 copy.19
  231.9 0.0 copy-start.1
  231.9 4.3 %copy.20 = bf16[512,3584]{1,0:T(8,128)(2,1)} copy(bf16[512,3584]{1,0:T(8,128)(2,1)} %get-tuple-element.9) | data formatting | bytes 7340032
  236.2 0.0 copy-done.1
  236.2 0.0 copy-start
  236.2 1.9 copy.21
  238.1 1.5 copy-done
  239.6 1.8 copy.22
Async XLA Ops:
  231.9 4.3 %copy-start.1 = (bf16[512,3584]{1,0:T(8,128)(2,1)S(1)}, bf16[512,3584]{1,0:T(8,128)(2,1)}, u32[]{:S(2)}) copy-start(bf16[512,3584]{1,0:T(8,128)(2,1)} %get-tuple-element.10) | copy-start | bytes 11010052
  236.2 3.4 %copy-start = (bf16[512,3584]{1,0:T(8,128)(2,1)S(1)}, bf16[512,3584]{1,0:T(8,128)(2,1)}, u32[]{:S(2)}) copy-start(bf16[512,3584]{1,0:T(8,128)(2,1)} %get-tuple-element.11) | copy-start | bytes 11010052

commit v2 on v1

v2 whole, which is shorter than its diff:
```python
import jax
import jax.numpy as jnp
from jax import lax
from jax.experimental import pallas as pl
from jax.experimental.pallas import tpu as pltpu
from jax.sharding import PartitionSpec as P

MESH = pl.DeviceIdType.MESH
BF16, F32 = jnp.bfloat16, jnp.float32
CAP = 8
TOK = 128
D = 3584
HDEV = 512
BLK = 16
ROWS = 256
HALF = 128
TILE = 512
NT = (((1,), (1,)), ((), ()))
NN = (((1,), (0,)), ((), ()))
STEPS = (
    (0, 0), (1, 0), (0, 1), (3, 0), (0, 3), (1, 1), (3, 3), (1, 3),
    (3, 1), (2, 0), (0, 2), (2, 1), (1, 2), (2, 3), (3, 2), (2, 2),
)
X_STEPS = sum(dx << (2 * q) for q, (dx, _) in enumerate(STEPS))
Y_STEPS = sum(dy << (2 * q) for q, (_, dy) in enumerate(STEPS))
PLACE = {0: (0, 128), 1: (256, 512), 3: (384, 640), 2: (768, 896)}
WHOLE = ((0, D),)
PIECES = ((0, 1536), (1536, 1024), (2560, 1024))


def signed(v):
    return v - (1 << 32) if v >= 1 << 31 else v


def mm(a, b, dims=NN):
    return lax.dot_general(a, b, dims, preferred_element_type=F32)


def mod4(v):
    return lax.rem(v, 4)


def tiled(body, start=0, size=D):
    def step(t, carry):
        body(pl.ds(pl.multiple_of(start + t * TILE, TILE), TILE))
        return carry

    lax.fori_loop(0, size // TILE, step, 0)


def place(d, q):
    return PLACE[d][q // 8] + q % 8 * BLK


def kernel(
    tok, cot, routes, slots, gates, wg_h, wu_h, wd_h,
    out_tok, og_h, ou_h, od_h,
    wg, wu, wd, xs, gs, snd, toks, cots, meta, onehot, picks, ret,
    swap_snd, swap_rcv, sum_snd, sum_rcv, ht, ggt, ugt, gg, ug, stage,
    w_sem, l_sem, cx_send, cx_recv, m_send, m_recv, own_sem, d_send, d_recv,
    z_send, z_recv, f_send, f_recv, r_send, r_recv, rown_sem,
    t_send, t_recv, o_send, o_recv, st_sem,
):
    node, local = lax.axis_index("node"), lax.axis_index("local")
    y, c = lax.div(node, 2), lax.rem(node, 2)
    x, z = lax.div(local, 4), lax.rem(local, 4)

    def dev(dx, dy, dz, flip=False):
        core = 1 - c if flip else c
        return (mod4(y + dy) * 2 + core, mod4(x + dx) * 4 + mod4(z + dz))

    def remote(src, dst, ssem, rsem, target):
        return pltpu.make_async_remote_copy(
            src_ref=src, dst_ref=dst, send_sem=ssem, recv_sem=rsem,
            device_id=target, device_id_type=MESH,
        )

    here = dev(0, 0, 0, True)

    def wait_recv(ref, sem):
        remote(ref, ref, sem, sem, here).wait_recv()

    def wait_send(ref, sem):
        remote(ref, ref, sem, sem, here).wait_send()

    mine = pl.ds(pl.multiple_of(c * TOK, TOK), TOK)
    own_loads = [
        pltpu.make_async_copy(src, dst.at[mine], l_sem.at[k])
        for k, (src, dst) in enumerate(((tok, toks), (cot, cots)))
    ]
    loads = [
        pltpu.make_async_copy(src, dst, w_sem.at[k])
        for k, (src, dst) in enumerate(((wg_h, wg), (wu_h, wu), (wd_h, wd)))
    ]
    for load in own_loads + loads:
        load.start()

    barrier = pltpu.get_barrier_semaphore()

    def greet(target):
        pl.semaphore_signal(barrier, inc=1, device_id=target, device_id_type=MESH)

    greet(here)
    for dx, dy in STEPS[1:]:
        greet(dev(dx, dy, 0))
    for dz in (1, 2, 3):
        greet(dev(0, 0, dz))

    line = lax.broadcasted_iota(jnp.int32, (8, TOK), 0)
    target = jnp.where(slots[...] < CAP, routes[...] * CAP + slots[...], -1).astype(F32)
    gate = gates[...]
    meta[0, c] = jnp.where(
        line == 0, target[0:1, :],
        jnp.where(line == 1, target[1:2, :], jnp.where(line == 2, gate[0:1, :], gate[1:2, :])),
    )
    pl.semaphore_wait(barrier, 19)

    swaps = [
        remote(src, dst, cx_send.at[k], cx_recv.at[k], here)
        for k, (src, dst) in enumerate(
            ((meta.at[0, c], meta.at[0, c]), (tok, toks.at[mine]), (cot, cots.at[mine]))
        )
    ]
    for swap in swaps:
        swap.start()

    def row_target(r, core):
        q2 = (r >> 4) * 2
        ey = mod4(y + ((jnp.int32(signed(Y_STEPS)) >> q2) & 3))
        ex = mod4(x + ((jnp.int32(signed(X_STEPS)) >> q2) & 3))
        e = (ey * 2 + c) * 4 + ex
        return jnp.where(((r >> 3) & 1) == core, e * CAP + (r & 7), -2).astype(F32)

    swaps[0].wait_recv()
    metas = [
        remote(meta.at[0], meta.at[4 - dz], m_send.at[dz - 1], m_recv.at[3 - dz], dev(0, 0, dz))
        for dz in (1, 2, 3)
    ]
    for m in metas:
        m.start()

    row_ids = lax.broadcasted_iota(jnp.int32, (ROWS, TOK), 0)
    row_gate = jnp.zeros((ROWS, 1), F32)
    for core in (0, 1):
        want = row_target(row_ids, core)
        mt = meta[0, core]
        hit0, hit1 = want == mt[0:1, :], want == mt[1:2, :]
        onehot[:, pl.ds(core * TOK, TOK)] = (
            jnp.where(hit0, 1.0, 0.0) + jnp.where(hit1, 1.0, 0.0)
        ).astype(BF16)
        picked = jnp.where(hit0, mt[2:3, :], 0.0) + jnp.where(hit1, mt[3:4, :], 0.0)
        row_gate = row_gate + jnp.sum(picked, axis=1, keepdims=True)

    for copy in own_loads:
        copy.wait()
    for swap in swaps[1:]:
        swap.wait_recv()

    bufs = (xs, gs)

    def own_copy(a):
        return pltpu.make_async_copy(
            snd.at[a, pl.ds(0, BLK)], bufs[a].at[pl.ds(0, BLK)], own_sem.at[a]
        )

    for half in range(2):
        rows = pl.ds(half * HALF, HALF)
        half_gate = row_gate[half * HALF : half * HALF + HALF]

        def build(cols, rows=rows, half_gate=half_gate):
            snd[0, rows, cols] = mm(onehot[rows, :], toks[:, cols]).astype(BF16)
            snd[1, rows, cols] = (half_gate * mm(onehot[rows, :], cots[:, cols])).astype(BF16)

        tiled(build)
        for q in range(half * 8, half * 8 + 8):
            dx, dy = STEPS[q]
            for a in range(2):
                if q == 0:
                    own_copy(a).start()
                else:
                    remote(
                        snd.at[a, pl.ds(q * BLK, BLK)], bufs[a].at[pl.ds(place(0, q), BLK)],
                        d_send.at[a], d_recv.at[q], dev(dx, dy, 0),
                    ).start()

    for q in range(16):
        if q == 0:
            for a in range(2):
                own_copy(a).wait()
        else:
            wait_recv(xs.at[pl.ds(0, 2 * BLK)], d_recv.at[q])
        for dz, slot in ((1, 3), (3, 1)):
            for a in range(2):
                remote(
                    bufs[a].at[pl.ds(place(0, q), BLK)], bufs[a].at[pl.ds(place(slot, q), BLK)],
                    z_send.at[dz // 2], z_recv.at[slot // 2, q], dev(0, 0, dz),
                ).start()

    def forward(q):
        for a, slot, dz in ((0, 3, 1), (1, 1, 3)):
            wait_recv(xs.at[pl.ds(0, 2 * BLK)], z_recv.at[slot // 2, q])
            remote(
                bufs[a].at[pl.ds(place(slot, q), BLK)], bufs[a].at[pl.ds(place(2, q), BLK)],
                f_send.at[a], f_recv.at[q], dev(0, 0, dz),
            ).start()

    def hidden_pass(row, count, at):
        rows, to = pl.ds(row, count), pl.ds(at, count)

        def step(h, carry):
            hid = pl.ds(pl.multiple_of(h * 256, 256), 256)
            pre_gate = mm(wg[hid, :], xs[rows, :], NT)
            pre_up = mm(wu[hid, :], xs[rows, :], NT)
            hidden_grad = mm(wd[hid, :], gs[rows, :], NT)
            sig = jax.nn.sigmoid(pre_gate)
            active = pre_gate * sig
            ht[hid, rows] = (active * pre_up).astype(BF16)
            gate_grad = hidden_grad * pre_up * sig * (1.0 + pre_gate * (1.0 - sig))
            up_grad = hidden_grad * active
            ggt[hid, rows] = gate_grad.astype(BF16)
            ugt[hid, rows] = up_grad.astype(BF16)
            gg[to, hid] = gate_grad.T.astype(BF16)
            ug[to, hid] = up_grad.T.astype(BF16)
            return carry

        lax.fori_loop(0, HDEV // 256, step, 0)

    def give_back(slot, at, count, blocks, sem, start=0, size=D):
        to = pl.ds(at, count)

        def part(cols):
            snd[slot, to, cols] = (
                mm(gg[to, :], wg[:, cols]) + mm(ug[to, :], wu[:, cols])
            ).astype(BF16)

        tiled(part, start, size)
        cols = pl.ds(start, size)
        own = []
        for row, d, q in blocks:
            src = snd.at[slot, pl.ds(row, BLK), cols]
            dst = ret.at[pl.ds(d * ROWS + q * BLK, BLK), cols]
            if q == 0:
                own.append(pltpu.make_async_copy(src, dst, rown_sem.at[d]))
                own[-1].start()
            else:
                dx, dy = STEPS[q]
                remote(
                    src, dst, r_send.at[sem], r_recv.at[d, sem], dev(4 - dx, 4 - dy, 0)
                ).start()
        for copy in own:
            copy.wait()

    def part_ids(d):
        return (3, 4, 5) if d == 2 else (d // 2 + (d > 0),)

    def spans(d):
        return PIECES if d == 2 else WHOLE

    def swap_copy(d, k):
        cols, i = pl.ds(*spans(d)[k]), part_ids(d)[k]
        return remote(
            swap_snd.at[d, :, cols], swap_rcv.at[d, :, cols], t_send.at[i], t_recv.at[i], here
        )

    def sum_copy(d, k):
        cols, i, o = pl.ds(*spans(d)[k]), part_ids(d)[k], part_ids((4 - d) % 4)[k]
        return remote(
            sum_snd.at[d, :, cols], sum_rcv.at[3 - d, :, cols],
            o_send.at[i], o_recv.at[o], dev(0, 0, d),
        )

    def prepare(d):
        if d:
            wait_recv(meta.at[d], m_recv.at[d - 1])
        col_ids = lax.broadcasted_iota(jnp.int32, (TOK, ROWS), 1)
        for k, core in enumerate((c, 1 - c)):
            want = row_target(col_ids, core)
            m = meta[d, core].T
            pick = jnp.where(want == m[:, 0:1], 1.0, 0.0) + jnp.where(want == m[:, 1:2], 1.0, 0.0)
            picks[d, k] = pick.astype(BF16)

    def combine(d, k):
        start, size = spans(d)[k]

        def sums(cols):
            rows = ret[pl.ds(d * ROWS, ROWS), cols]
            sum_snd[d, :, cols] = mm(picks[d, 0], rows).astype(BF16)
            swap_snd[d, :, cols] = mm(picks[d, 1], rows).astype(BF16)

        tiled(sums, start, size)
        swap_copy(d, k).start()

    def pass_on(d, k):
        start, size = spans(d)[k]
        swap_copy(d, k).wait_recv()

        def add(cols):
            both = sum_snd[d, :, cols].astype(F32) + swap_rcv[d, :, cols].astype(F32)
            sum_snd[d, :, cols] = both.astype(BF16)

        tiled(add, start, size)
        if d:
            sum_copy(d, k).start()

    def wait_back(d, rows, sem, start=0, size=D):
        wait_recv(ret.at[pl.ds(0, rows), pl.ds(start, size)], r_recv.at[d, sem])

    for q in range(8):
        forward(q)
    for load in loads:
        load.wait()
    for a in range(2):
        wait_send(snd.at[a, pl.ds(0, 240)], d_send.at[a])
    hidden_pass(0, ROWS, 0)
    give_back(0, 0, ROWS, [(q * BLK, 0, q) for q in range(16)], 0)
    hidden_pass(256, ROWS, 0)
    near = [(q % 8 * BLK + k * HALF, d, q) for k, d in enumerate((1, 3)) for q in range(16)]
    give_back(1, 0, ROWS, [b for b in near if b[2] < 8], 1)
    for d in range(4):
        prepare(d)
    for q in range(8, 16):
        forward(q)

    wait_send(snd.at[0, pl.ds(0, 240)], r_send.at[0])
    hidden_pass(512, ROWS, 0)
    give_back(0, 0, ROWS, [b for b in near if b[2] >= 8], 2)
    wait_back(0, 240, 0)
    combine(0, 0)

    for q in range(8):
        wait_recv(xs.at[pl.ds(0, 2 * BLK)], f_recv.at[q])
    pass_on(0, 0)
    wait_send(snd.at[1, pl.ds(0, 224)], r_send.at[1])
    hidden_pass(768, HALF, 0)
    give_back(1, 0, HALF, [(q * BLK, 2, q) for q in range(8)], 3)
    for d in (1, 3):
        wait_back(d, 112, 1)
        wait_back(d, 128, 2)
        combine(d, 0)
    for d in (1, 3):
        pass_on(d, 0)
    for q in range(8, 16):
        wait_recv(xs.at[pl.ds(0, 2 * BLK)], f_recv.at[q])
    hidden_pass(896, HALF, HALF)
    for k, span in enumerate(PIECES):
        give_back(1, HALF, HALF, [(q * BLK, 2, q) for q in range(8, 16)], 4 + k, *span)

    jobs = ((ggt, xs, og_h), (ugt, xs, ou_h), (ht, gs, od_h))

    def stage_copy(t, n):
        return pltpu.make_async_copy(
            stage.at[t % 2, n], jobs[n][2].at[:, pl.ds(t * TILE, TILE)], st_sem.at[t % 2, n]
        )

    def wgrad(t):
        for n, (left, right, _) in enumerate(jobs):
            if t >= 2:
                stage_copy(t - 2, n).wait()
            stage[t % 2, n] = mm(left[...], right[:, pl.ds(t * TILE, TILE)]).astype(BF16)
            stage_copy(t, n).start()

    def last(k):
        if k == 0:
            wait_back(2, 112, 3)
        wait_back(2, 128, 4 + k, *PIECES[k])
        combine(2, k)

    wgrad(0)
    wgrad(1)
    wgrad(2)
    last(0)
    wgrad(3)
    pass_on(2, 0)
    last(1)
    wgrad(4)
    pass_on(2, 1)
    last(2)
    wgrad(5)
    pass_on(2, 2)
    wgrad(6)

    for d in (1, 3):
        wait_recv(sum_rcv.at[d - 1], o_recv.at[part_ids(d)[0]])
    for k, (start, size) in enumerate(PIECES):
        wait_recv(sum_rcv.at[1, :, pl.ds(start, size)], o_recv.at[part_ids(2)[k]])

        def total(cols):
            acc = sum_snd[0, :, cols].astype(F32)
            for n in range(3):
                acc = acc + sum_rcv[n, :, cols].astype(F32)
            out_tok[:, cols] = acc.astype(BF16)

        tiled(total, start, size)

    for t in (5, 6):
        for n in range(3):
            stage_copy(t, n).wait()
    for swap in swaps:
        swap.wait_send()
    for m in metas:
        m.wait_send()
    for k in range(2):
        wait_send(xs.at[pl.ds(0, 512)], z_send.at[k])
        wait_send(xs.at[pl.ds(0, ROWS)], f_send.at[k])
    wait_send(snd.at[0, pl.ds(0, ROWS)], r_send.at[2])
    wait_send(snd.at[0, pl.ds(0, 112)], r_send.at[3])
    for k, (start, size) in enumerate(PIECES):
        wait_send(snd.at[0, pl.ds(0, HALF), pl.ds(start, size)], r_send.at[4 + k])
    for d in range(4):
        for k in range(len(spans(d))):
            swap_copy(d, k).wait_send()
            if d:
                sum_copy(d, k).wait_send()


def per_device(tokens, cotangent, routes, route_gates, route_slots, w_gate, w_up, w_down):
    vmem, hbm = pl.BlockSpec(memory_space=pltpu.VMEM), pl.BlockSpec(memory_space=pl.ANY)
    dma = pltpu.SemaphoreType.DMA
    grad = jax.ShapeDtypeStruct((HDEV, D), BF16)

    def room(*shape):
        return pltpu.VMEM(shape, BF16)

    return pl.pallas_call(
        kernel,
        out_shape=(jax.ShapeDtypeStruct((TOK, D), BF16), grad, grad, grad),
        in_specs=[hbm] * 2 + [vmem] * 3 + [hbm] * 3,
        out_specs=(vmem, hbm, hbm, hbm),
        scratch_shapes=[
            room(HDEV, D), room(HDEV, D), room(HDEV, D),
            room(4 * ROWS, D), room(4 * ROWS, D), room(2, ROWS, D),
            room(2 * TOK, D), room(2 * TOK, D),
            pltpu.VMEM((4, 2, 8, TOK), F32), room(ROWS, 2 * TOK), room(4, 2, TOK, ROWS),
            room(4 * ROWS, D),
            room(4, TOK, D), room(4, TOK, D), room(4, TOK, D), room(3, TOK, D),
            room(HDEV, 4 * ROWS), room(HDEV, 4 * ROWS), room(HDEV, 4 * ROWS),
            room(ROWS, HDEV), room(ROWS, HDEV), room(2, 3, HDEV, TILE),
            dma((3,)), dma((2,)), dma((3,)), dma((3,)), dma((3,)), dma((3,)), dma((2,)),
            dma((2,)), dma((16,)),
            dma((2,)), dma((2, 16)), dma((2,)), dma((16,)), dma((7,)), dma((4, 7)), dma((4,)),
            dma((6,)), dma((6,)), dma((6,)), dma((6,)), dma((2, 3)),
        ],
        compiler_params=pltpu.CompilerParams(
            collective_id=0, has_side_effects=True, vmem_limit_bytes=63 * 2**20
        ),
        cost_estimate=pl.CostEstimate(
            flops=8 * 2 * 1024 * D * HDEV, bytes_accessed=6 * 2 * HDEV * D, transcendentals=1024 * HDEV
        ),
    )(tokens, cotangent, routes.T, route_slots.T, route_gates.T, w_gate, w_up, w_down)


def solution(mesh):
    spec = P(("node", "local"), None)
    return jax.shard_map(
        per_device, mesh=mesh, in_specs=(spec,) * 8, out_specs=(spec,) * 4, check_vma=False
    )
```

time: 244 us -> 206 us (0.84); the launches traced: 241 us -> 206 us
  Pallas kernels: 225 us -> 194 us
  local copies, waits for them, and re-layouts: 15.9 us -> 11.6 us
    pallas_call x1, Pallas kernels: 225 us -> 194 us  [per_device(): pl.pallas_call(kernel, out_shape=(jax.ShapeDtypeStruct((TOK, D), BF16), g...]
    unnamed x11 -> x8, local copies, waits for them, and re-layouts: 15.9 us -> 11.6 us
where the time goes in v2:
time: 206 us
  Pallas kernels  194 us (94%)
  local copies, waits for them, and re-layouts  11.6 us (6%)
    pallas_call x1, Pallas kernels, per_device(): pl.pallas_call(kernel, out_shape=(jax.ShapeDtypeStruct((TOK, D), BF16), g...  194 us
    unnamed x8, local copies, waits for them, and re-layouts  11.6 us

profile of v2, /device:TPU:26, one launch (start us, length us, event | category | flops | bytes accessed | tf_op | source)
XLA Modules:
  0.0 206.1 jit_solution(10076983186924089814)
XLA Ops:
  0.6 193.9 %shard_map.111 = (bf16[128,3584]{1,0:T(8,128)(2,1)}, bf16[512,3584]{1,0:T(8,128)(2,1)}, bf16[512,3584]{1,0:T(8,128)(2,1)}, bf16[512,3584]{1,0:T(8,128)(2,1)}) custom-call(bf16[128,3584]{1,0:T(8,128)(2,1)} %tok.1, bf16[128,3584]{1,0:T(8,128)(2,1)} %cot.1, s32[2,128]{1,0:T(2,128)} %bitcast.3, s32[2,128]{1,0:T(2,128)} %bitcast.4, f32[2,128]{1,0:T(2,128)} %bitcast.5, ...), custom_call_target="tpu_custom_call" | custom-call | flops 30064771072 | bytes 22020096 | tf_op jit(solution)/shard_map/pallas_call | solution.py:424
  194.5 2.2 %copy.16 = bf16[128,3584]{1,0:T(8,128)(2,1)} copy(bf16[128,3584]{1,0:T(8,128)(2,1)} %get-tuple-element.8) | data formatting | bytes 1835008
  196.7 0.0 copy-start.1
  196.7 4.3 %copy.17 = bf16[512,3584]{1,0:T(8,128)(2,1)} copy(bf16[512,3584]{1,0:T(8,128)(2,1)} %get-tuple-element.9) | data formatting | bytes 7340032
  200.9 0.0 copy-done.1
  200.9 0.0 copy-start
  200.9 1.9 copy.18
  202.8 1.5 copy-done
  204.3 1.8 copy.19
Async XLA Ops:
  196.7 4.3 %copy-start.1 = (bf16[512,3584]{1,0:T(8,128)(2,1)S(1)}, bf16[512,3584]{1,0:T(8,128)(2,1)}, u32[]{:S(2)}) copy-start(bf16[512,3584]{1,0:T(8,128)(2,1)} %get-tuple-element.10) | copy-start | bytes 11010052
  200.9 3.4 %copy-start = (bf16[512,3584]{1,0:T(8,128)(2,1)S(1)}, bf16[512,3584]{1,0:T(8,128)(2,1)}, u32[]{:S(2)}) copy-start(bf16[512,3584]{1,0:T(8,128)(2,1)} %get-tuple-element.11) | copy-start | bytes 11010052

commit v3 on v2

--- a/solution.py
+++ b/solution.py
@@ -54,7 +54,7 @@
 
 def kernel(
     tok, cot, routes, slots, gates, wg_h, wu_h, wd_h,
-    out_tok, og_h, ou_h, od_h,
+    out_tok, out_last, out_rest, og_h, ou_h, od_h,
     wg, wu, wd, xs, gs, snd, toks, cots, meta, onehot, picks, ret,
     swap_snd, swap_rcv, sum_snd, sum_rcv, ht, ggt, ugt, gg, ug, stage,
     w_sem, l_sem, cx_send, cx_recv, m_send, m_recv, own_sem, d_send, d_recv,
@@ -262,6 +262,9 @@
             swap_snd.at[d, :, cols], swap_rcv.at[d, :, cols], t_send.at[i], t_recv.at[i], here
         )
 
+    def stays(d, k):
+        return d > 0 and (d, k) != (2, 2)
+
     def sum_copy(d, k):
         cols, i, o = pl.ds(*spans(d)[k]), part_ids(d)[k], part_ids((4 - d) % 4)[k]
         return remote(
@@ -298,8 +301,13 @@
             both = sum_snd[d, :, cols].astype(F32) + swap_rcv[d, :, cols].astype(F32)
             sum_snd[d, :, cols] = both.astype(BF16)
 
+        if (d, k) == (2, 2):
+            def add(cols):
+                both = sum_snd[d, :, cols].astype(F32) + swap_rcv[d, :, cols].astype(F32)
+                out_last[:, pl.ds(cols.start - start, TILE)] = both.astype(BF16)
+
         tiled(add, start, size)
-        if d:
+        if stays(d, k):
             sum_copy(d, k).start()
 
     def wait_back(d, rows, sem, start=0, size=D):
@@ -382,13 +390,17 @@
     for d in (1, 3):
         wait_recv(sum_rcv.at[d - 1], o_recv.at[part_ids(d)[0]])
     for k, (start, size) in enumerate(PIECES):
-        wait_recv(sum_rcv.at[1, :, pl.ds(start, size)], o_recv.at[part_ids(2)[k]])
-
-        def total(cols):
+        if k < 2:
+            wait_recv(sum_rcv.at[1, :, pl.ds(start, size)], o_recv.at[part_ids(2)[k]])
+
+        def total(cols, k=k):
             acc = sum_snd[0, :, cols].astype(F32)
-            for n in range(3):
+            for n in (0, 1, 2) if k < 2 else (0, 2):
                 acc = acc + sum_rcv[n, :, cols].astype(F32)
-            out_tok[:, cols] = acc.astype(BF16)
+            if k < 2:
+                out_tok[:, cols] = acc.astype(BF16)
+            else:
+                out_rest[:, pl.ds(cols.start - start, TILE)] = acc
 
         tiled(total, start, size)
 
@@ -409,8 +421,26 @@
     for d in range(4):
         for k in range(len(spans(d))):
             swap_copy(d, k).wait_send()
-            if d:
+            if stays(d, k):
                 sum_copy(d, k).wait_send()
+
+
+def hand_over(a_in, b_in, c_in, a_out, b_out, c_out, held, in_sem, out_sem):
+    ways = []
+    for n, (src, dst) in enumerate(((a_in, a_out), (b_in, b_out), (c_in, c_out))):
+        for k in range(4):
+            rows, slot = pl.ds(k * HALF, HALF), held.at[n, k]
+            ways.append((
+                pltpu.make_async_copy(src.at[rows], slot, in_sem.at[n, k]),
+                pltpu.make_async_copy(slot, dst.at[rows], out_sem.at[n, k]),
+            ))
+    for enter, _ in ways:
+        enter.start()
+    for enter, leave in ways:
+        enter.wait()
+        leave.start()
+    for _, leave in ways:
+        leave.wait()
 
 
 def per_device(tokens, cotangent, routes, route_gates, route_slots, w_gate, w_up, w_down):
@@ -421,11 +451,17 @@
     def room(*shape):
         return pltpu.VMEM(shape, BF16)
 
-    return pl.pallas_call(
+    start, size = PIECES[2]
+    done, last, rest, *grads = pl.pallas_call(
         kernel,
-        out_shape=(jax.ShapeDtypeStruct((TOK, D), BF16), grad, grad, grad),
+        out_shape=(
+            jax.ShapeDtypeStruct((TOK, start), BF16),
+            jax.ShapeDtypeStruct((TOK, size), BF16),
+            jax.ShapeDtypeStruct((TOK, size), F32),
+            grad, grad, grad,
+        ),
         in_specs=[hbm] * 2 + [vmem] * 3 + [hbm] * 3,
-        out_specs=(vmem, hbm, hbm, hbm),
+        out_specs=(vmem, vmem, vmem, hbm, hbm, hbm),
         scratch_shapes=[
             room(HDEV, D), room(HDEV, D), room(HDEV, D),
             room(4 * ROWS, D), room(4 * ROWS, D), room(2, ROWS, D),
@@ -447,6 +483,21 @@
             flops=8 * 2 * 1024 * D * HDEV, bytes_accessed=6 * 2 * HDEV * D, transcendentals=1024 * HDEV
         ),
     )(tokens, cotangent, routes.T, route_slots.T, route_gates.T, w_gate, w_up, w_down)
+    opposite = [(i, i // 4 * 4 + (i + 2) % 4) for i in range(16)]
+    far = lax.ppermute(last, "local", opposite)
+    grads = pl.pallas_call(
+        hand_over,
+        out_shape=(grad, grad, grad),
+        in_specs=[hbm] * 3,
+        out_specs=[hbm] * 3,
+        scratch_shapes=[room(3, 4, HALF, D), dma((3, 4)), dma((3, 4))],
+        compiler_params=pltpu.CompilerParams(vmem_limit_bytes=63 * 2**20),
+        cost_estimate=pl.CostEstimate(
+            flops=0, bytes_accessed=6 * 2 * HDEV * D, transcendentals=0
+        ),
+    )(*grads)
+    tail = (rest + far.astype(F32)).astype(BF16)
+    return (jnp.concatenate([done, tail], axis=1), *grads)
 
 
 def solution(mesh):

time: 206 us -> 200 us (0.971)
  local copies, waits for them, and re-layouts: 11.6 us -> 0.01 us
  other arithmetic: 0 us -> 2.08 us
    unnamed x8 -> x2, local copies, waits for them, and re-layouts: 11.6 us -> 0.01 us
    pallas_call x1 -> x2, Pallas kernels: 194 us -> 195 us  [the longest x1 186 us: per_device(): pl.pallas_call(kernel, out_shape=(jax.ShapeDtypeStruct((TOK, start), BF16...]
  transfers between devices with their start and end apart: 0 -> 1, of which waited for: 0 -> 1; matrix products, arithmetic and copies ran while one was open for 0% -> 0% of each run, Pallas kernels for 0% -> 4%
where the time goes in v3:
time: 200 us; the launch traced here: 199 us
  Pallas kernels  195 us (98%)
  other arithmetic  2.08 us (1%)
    pallas_call x1, Pallas kernels, per_device(): pl.pallas_call(kernel, out_shape=(jax.ShapeDtypeStruct((TOK, start), BF16...  186 us
    pallas_call x1, Pallas kernels, per_device(): pl.pallas_call(hand_over, out_shape=(grad, grad, grad), in_specs=[hbm] *...  8.64 us
  transfers between devices with their start and end apart: 1, of which 1 were waited for; matrix products, arithmetic and copies ran while one was open for 0% of the time, Pallas kernels for 4%

profile of v3, /device:TPU:26, one launch (start us, length us, event | category | flops | bytes accessed | tf_op | source)
XLA Modules:
  0.0 199.0 jit_solution(11830797133868024266)
XLA Ops:
  0.6 186.1 %shard_map.111 = (bf16[128,2560]{1,0:T(8,128)(2,1)}, bf16[128,1024]{1,0:T(8,128)(2,1)}, f32[128,1024]{1,0:T(8,128)}, bf16[512,3584]{1,0:T(8,128)(2,1)}, bf16[512...) custom-call(bf16[128,3584]{1,0:T(8,128)(2,1)} %tok.1, bf16[128,3584]{1,0:T(8,128)(2,1)} %cot.1, s32[2,128]{1,0:T(2,128)} %bitcast.3, ...), custom_call_target="tpu_custom_call" | custom-call | flops 30064771072 | bytes 22020096 | tf_op jit(solution)/shard_map/pallas_call | solution.py:455
  186.7 0.6 collective-permute-start
  187.4 0.0 copy-start
  187.4 8.6 %shard_map.112 = (bf16[512,3584]{1,0:T(8,128)(2,1)}, bf16[512,3584]{1,0:T(8,128)(2,1)}, bf16[512,3584]{1,0:T(8,128)(2,1)}) custom-call(bf16[512,3584]{1,0:T(8,128)(2,1)} %get-tuple-element.16.a_in, bf16[512,3584]{1,0:T(8,128)(2,1)} %get-tuple-element.17.b_in, bf16[512,3584]{1,0:T(8,128)(2,1)} %get-tuple-element.18.c_in), custom_call_target="tpu_custom_call" | custom-call | bytes 22020096 | tf_op jit(solution)/shard_map/pallas_call | solution.py:488
  196.0 0.8 collective-permute-done
  196.9 1.1 add_convert_fusion
  198.0 0.0 copy-done
  198.0 1.0 pad_maximum_fusion
Async XLA Ops:
  186.7 10.1 %collective-permute-start = (bf16[128,1024]{1,0:T(8,128)(2,1)}, bf16[128,1024]{1,0:T(8,128)(2,1)S(1)}, u32[]{:S(2)}, u32[]{:S(2)}) collective-permute-start(bf16[128,1024]{1,0:T(8,128)(2,1)} %get-tuple-element.15), channel_id=1, source_target_pairs={{0,2},{1,3},{2,0},{3,1},{4,6},{5,7},{6,4},{7,5},{8,10},{9,11},{10,... | collective-permute-start | bytes 786440 | tf_op jit(solution)/shard_map/ppermute | solution.py:487
  187.4 10.6 %copy-start = (bf16[128,2560]{1,0:T(8,128)(2,1)S(1)}, bf16[128,2560]{1,0:T(8,128)(2,1)}, u32[]{:S(2)}) copy-start(bf16[128,2560]{1,0:T(8,128)(2,1)} %get-tuple-element.13) | copy-start | bytes 1966084

commit v4 on v3

--- a/solution.py
+++ b/solution.py
@@ -23,9 +23,10 @@
 )
 X_STEPS = sum(dx << (2 * q) for q, (dx, _) in enumerate(STEPS))
 Y_STEPS = sum(dy << (2 * q) for q, (_, dy) in enumerate(STEPS))
-PLACE = {0: (0, 128), 1: (256, 512), 3: (384, 640), 2: (768, 896)}
 WHOLE = ((0, D),)
 PIECES = ((0, 1536), (1536, 1024), (2560, 1024))
+LEAVE = 2560
+ENTRY = ((0, 1536), (1536, 2048))
 
 
 def signed(v):
@@ -49,7 +50,11 @@
 
 
 def place(d, q):
-    return PLACE[d][q // 8] + q % 8 * BLK
+    if d in (0, 2):
+        return d * 384 + q * BLK
+    if q < 8:
+        return 256 + d // 2 * HALF + q * BLK
+    return 512 + (q - 8) // 4 * HALF + d // 2 * 64 + q % 4 * BLK
 
 
 def kernel(
@@ -118,7 +123,12 @@
     swaps = [
         remote(src, dst, cx_send.at[k], cx_recv.at[k], here)
         for k, (src, dst) in enumerate(
-            ((meta.at[0, c], meta.at[0, c]), (tok, toks.at[mine]), (cot, cots.at[mine]))
+            [(meta.at[0, c], meta.at[0, c])]
+            + [
+                (src.at[:, pl.ds(*span)], dst.at[mine, pl.ds(*span)])
+                for span in ENTRY
+                for src, dst in ((tok, toks), (cot, cots))
+            ]
         )
     ]
     for swap in swaps:
@@ -153,9 +163,6 @@
 
     for copy in own_loads:
         copy.wait()
-    for swap in swaps[1:]:
-        swap.wait_recv()
-
     bufs = (xs, gs)
 
     def own_copy(a):
@@ -171,7 +178,11 @@
             snd[0, rows, cols] = mm(onehot[rows, :], toks[:, cols]).astype(BF16)
             snd[1, rows, cols] = (half_gate * mm(onehot[rows, :], cots[:, cols])).astype(BF16)
 
-        tiled(build)
+        for n, span in enumerate(ENTRY):
+            if half == 0:
+                for swap in swaps[1 + 2 * n : 3 + 2 * n]:
+                    swap.wait_recv()
+            tiled(build, *span)
         for q in range(half * 8, half * 8 + 8):
             dx, dy = STEPS[q]
             for a in range(2):
@@ -190,15 +201,20 @@
         else:
             wait_recv(xs.at[pl.ds(0, 2 * BLK)], d_recv.at[q])
         for dz, slot in ((1, 3), (3, 1)):
+            if q >= 8:
+                wait_send(xs.at[pl.ds(0, 2 * BLK)], z_send.at[dz // 2, q - 8])
             for a in range(2):
                 remote(
                     bufs[a].at[pl.ds(place(0, q), BLK)], bufs[a].at[pl.ds(place(slot, q), BLK)],
-                    z_send.at[dz // 2], z_recv.at[slot // 2, q], dev(0, 0, dz),
+                    z_send.at[dz // 2, q], z_recv.at[slot // 2, q], dev(0, 0, dz),
                 ).start()
+
+    def wait_near(q):
+        for k in range(2):
+            wait_recv(xs.at[pl.ds(0, 2 * BLK)], z_recv.at[k, q])
 
     def forward(q):
         for a, slot, dz in ((0, 3, 1), (1, 1, 3)):
-            wait_recv(xs.at[pl.ds(0, 2 * BLK)], z_recv.at[slot // 2, q])
             remote(
                 bufs[a].at[pl.ds(place(slot, q), BLK)], bufs[a].at[pl.ds(place(2, q), BLK)],
                 f_send.at[a], f_recv.at[q], dev(0, 0, dz),
@@ -293,7 +309,7 @@
         tiled(sums, start, size)
         swap_copy(d, k).start()
 
-    def pass_on(d, k):
+    def pass_on(d, k, send=True):
         start, size = spans(d)[k]
         swap_copy(d, k).wait_recv()
 
@@ -302,56 +318,66 @@
             sum_snd[d, :, cols] = both.astype(BF16)
 
         if (d, k) == (2, 2):
+
             def add(cols):
                 both = sum_snd[d, :, cols].astype(F32) + swap_rcv[d, :, cols].astype(F32)
-                out_last[:, pl.ds(cols.start - start, TILE)] = both.astype(BF16)
+                out_last[:, pl.ds(cols.start - LEAVE, TILE)] = both.astype(BF16)
 
         tiled(add, start, size)
-        if stays(d, k):
+        if send and stays(d, k):
             sum_copy(d, k).start()
 
     def wait_back(d, rows, sem, start=0, size=D):
         wait_recv(ret.at[pl.ds(0, rows), pl.ds(start, size)], r_recv.at[d, sem])
 
-    for q in range(8):
-        forward(q)
     for load in loads:
         load.wait()
     for a in range(2):
         wait_send(snd.at[a, pl.ds(0, 240)], d_send.at[a])
-    hidden_pass(0, ROWS, 0)
-    give_back(0, 0, ROWS, [(q * BLK, 0, q) for q in range(16)], 0)
+    for q in range(8):
+        wait_near(q)
     hidden_pass(256, ROWS, 0)
-    near = [(q % 8 * BLK + k * HALF, d, q) for k, d in enumerate((1, 3)) for q in range(16)]
-    give_back(1, 0, ROWS, [b for b in near if b[2] < 8], 1)
+    near = [(place(d, q), d, q) for d in (1, 3) for q in range(16)]
+    give_back(1, 0, ROWS, [(row - 256, d, q) for row, d, q in near if row < 512], 1)
     for d in range(4):
         prepare(d)
-    for q in range(8, 16):
+
+    for q in range(8, 12):
+        wait_near(q)
+    hidden_pass(512, HALF, 0)
+    give_back(0, 0, HALF, [(row - 512, d, q) for row, d, q in near if 512 <= row < 640], 2)
+    hidden_pass(0, HALF, HALF)
+    wait_send(snd.at[1, pl.ds(0, 224)], r_send.at[1])
+    give_back(1, HALF, HALF, [(HALF + q * BLK, 0, q) for q in range(8)], 0)
+    for q in range(12, 16):
+        wait_near(q)
+        if q >= 14:
+            forward(q - 14)
+    for q in range(2, 16):
         forward(q)
-
-    wait_send(snd.at[0, pl.ds(0, 240)], r_send.at[0])
-    hidden_pass(512, ROWS, 0)
-    give_back(0, 0, ROWS, [b for b in near if b[2] >= 8], 2)
-    wait_back(0, 240, 0)
-    combine(0, 0)
+    hidden_pass(640, HALF, HALF)
+    give_back(0, HALF, HALF, [(row - 512, d, q) for row, d, q in near if row >= 640], 7)
+    hidden_pass(HALF, HALF, 0)
+    give_back(1, 0, HALF, [(q * BLK - HALF, 0, q) for q in range(8, 16)], 8)
 
     for q in range(8):
         wait_recv(xs.at[pl.ds(0, 2 * BLK)], f_recv.at[q])
-    pass_on(0, 0)
-    wait_send(snd.at[1, pl.ds(0, 224)], r_send.at[1])
     hidden_pass(768, HALF, 0)
-    give_back(1, 0, HALF, [(q * BLK, 2, q) for q in range(8)], 3)
+    wait_send(snd.at[0, pl.ds(0, HALF)], r_send.at[2])
+    give_back(0, 0, HALF, [(q * BLK, 2, q) for q in range(8)], 3)
     for d in (1, 3):
         wait_back(d, 112, 1)
-        wait_back(d, 128, 2)
+        wait_back(d, 64, 2)
+        wait_back(d, 64, 7)
         combine(d, 0)
     for d in (1, 3):
         pass_on(d, 0)
     for q in range(8, 16):
         wait_recv(xs.at[pl.ds(0, 2 * BLK)], f_recv.at[q])
     hidden_pass(896, HALF, HALF)
+    wait_send(snd.at[0, pl.ds(0, HALF)], r_send.at[7])
     for k, span in enumerate(PIECES):
-        give_back(1, HALF, HALF, [(q * BLK, 2, q) for q in range(8, 16)], 4 + k, *span)
+        give_back(0, HALF, HALF, [(q * BLK, 2, q) for q in range(8, 16)], 4 + k, *span)
 
     jobs = ((ggt, xs, og_h), (ugt, xs, ou_h), (ht, gs, od_h))
 
@@ -374,7 +400,11 @@
         combine(2, k)
 
     wgrad(0)
+    wait_back(0, 112, 0)
+    wait_back(0, 128, 8)
+    combine(0, 0)
     wgrad(1)
+    pass_on(0, 0)
     wgrad(2)
     last(0)
     wgrad(3)
@@ -383,25 +413,27 @@
     wgrad(4)
     pass_on(2, 1)
     last(2)
+    pass_on(2, 2)
     wgrad(5)
-    pass_on(2, 2)
     wgrad(6)
 
     for d in (1, 3):
         wait_recv(sum_rcv.at[d - 1], o_recv.at[part_ids(d)[0]])
-    for k, (start, size) in enumerate(PIECES):
-        if k < 2:
-            wait_recv(sum_rcv.at[1, :, pl.ds(start, size)], o_recv.at[part_ids(2)[k]])
-
-        def total(cols, k=k):
-            acc = sum_snd[0, :, cols].astype(F32)
-            for n in (0, 1, 2) if k < 2 else (0, 2):
-                acc = acc + sum_rcv[n, :, cols].astype(F32)
-            if k < 2:
-                out_tok[:, cols] = acc.astype(BF16)
-            else:
-                out_rest[:, pl.ds(cols.start - start, TILE)] = acc
-
+
+    def others(cols):
+        acc = sum_snd[0, :, cols].astype(F32) + sum_rcv[0, :, cols].astype(F32)
+        return acc + sum_rcv[2, :, cols].astype(F32)
+
+    def rest(cols):
+        out_rest[:, pl.ds(cols.start - LEAVE, TILE)] = others(cols)
+
+    def total(cols):
+        out_tok[:, cols] = (others(cols) + sum_rcv[1, :, cols].astype(F32)).astype(BF16)
+
+    tiled(rest, LEAVE, D - LEAVE)
+    for k in range(2):
+        start, size = PIECES[k]
+        wait_recv(sum_rcv.at[1, :, pl.ds(start, size)], o_recv.at[part_ids(2)[k]])
         tiled(total, start, size)
 
     for t in (5, 6):
@@ -412,9 +444,11 @@
     for m in metas:
         m.wait_send()
     for k in range(2):
-        wait_send(xs.at[pl.ds(0, 512)], z_send.at[k])
+        for q in range(8, 16):
+            wait_send(xs.at[pl.ds(0, 2 * BLK)], z_send.at[k, q])
         wait_send(xs.at[pl.ds(0, ROWS)], f_send.at[k])
-    wait_send(snd.at[0, pl.ds(0, ROWS)], r_send.at[2])
+    wait_send(snd.at[0, pl.ds(0, 112)], r_send.at[0])
+    wait_send(snd.at[0, pl.ds(0, HALF)], r_send.at[8])
     wait_send(snd.at[0, pl.ds(0, 112)], r_send.at[3])
     for k, (start, size) in enumerate(PIECES):
         wait_send(snd.at[0, pl.ds(0, HALF), pl.ds(start, size)], r_send.at[4 + k])
@@ -451,7 +485,7 @@
     def room(*shape):
         return pltpu.VMEM(shape, BF16)
 
-    start, size = PIECES[2]
+    start, size = LEAVE, D - LEAVE
     done, last, rest, *grads = pl.pallas_call(
         kernel,
         out_shape=(
@@ -471,9 +505,9 @@
             room(4, TOK, D), room(4, TOK, D), room(4, TOK, D), room(3, TOK, D),
             room(HDEV, 4 * ROWS), room(HDEV, 4 * ROWS), room(HDEV, 4 * ROWS),
             room(ROWS, HDEV), room(ROWS, HDEV), room(2, 3, HDEV, TILE),
-            dma((3,)), dma((2,)), dma((3,)), dma((3,)), dma((3,)), dma((3,)), dma((2,)),
+            dma((3,)), dma((2,)), dma((5,)), dma((5,)), dma((3,)), dma((3,)), dma((2,)),
             dma((2,)), dma((16,)),
-            dma((2,)), dma((2, 16)), dma((2,)), dma((16,)), dma((7,)), dma((4, 7)), dma((4,)),
+            dma((2, 16)), dma((2, 16)), dma((2,)), dma((16,)), dma((9,)), dma((4, 9)), dma((4,)),
             dma((6,)), dma((6,)), dma((6,)), dma((6,)), dma((2, 3)),
         ],
         compiler_params=pltpu.CompilerParams(
@@ -496,8 +530,9 @@
             flops=0, bytes_accessed=6 * 2 * HDEV * D, transcendentals=0
         ),
     )(*grads)
-    tail = (rest + far.astype(F32)).astype(BF16)
-    return (jnp.concatenate([done, tail], axis=1), *grads)
+    tail = jnp.pad(rest + far.astype(F32), ((0, 0), (start, 0)))
+    total = jnp.pad(done.astype(F32), ((0, 0), (0, size))) + tail
+    return (total.astype(BF16), *grads)
 
 
 def solution(mesh):

time: 200 us -> 198 us (0.990); the launches traced: 199 us -> 195 us
  Pallas kernels: 195 us -> 192 us
    pallas_call x1, Pallas kernels: 186 us -> 183 us  [per_device(): pl.pallas_call(kernel, out_shape=(jax.ShapeDtypeStruct((TOK, start), BF16...]
  transfers between devices with their start and end apart: 1 -> 1, of which waited for: 1 -> 0; matrix products, arithmetic and copies ran while one was open for 0% -> 0% of each run, Pallas kernels for 4% -> 4%
where the time goes in v4:
time: 198 us; the launch traced here: 195 us
  Pallas kernels  192 us (97%)
  other arithmetic  2.09 us (1%)
    pallas_call x1, Pallas kernels, per_device(): pl.pallas_call(kernel, out_shape=(jax.ShapeDtypeStruct((TOK, start), BF16...  183 us
    pallas_call x1, Pallas kernels, per_device(): pl.pallas_call(hand_over, out_shape=(grad, grad, grad), in_specs=[hbm] *...  8.64 us
  transfers between devices with their start and end apart: 1, of which 0 were waited for; matrix products, arithmetic and copies ran while one was open for 0% of the time, Pallas kernels for 4%

profile of v4, /device:TPU:26, one launch (start us, length us, event | category | flops | bytes accessed | tf_op | source)
XLA Modules:
  0.0 194.8 jit_solution(2476152574463481013)
XLA Ops:
  0.6 182.9 %shard_map.111 = (bf16[128,2560]{1,0:T(8,128)(2,1)}, bf16[128,1024]{1,0:T(8,128)(2,1)}, f32[128,1024]{1,0:T(8,128)}, bf16[512,3584]{1,0:T(8,128)(2,1)}, bf16[512...) custom-call(bf16[128,3584]{1,0:T(8,128)(2,1)} %tok.1, bf16[128,3584]{1,0:T(8,128)(2,1)} %cot.1, s32[2,128]{1,0:T(2,128)} %bitcast.3, ...), custom_call_target="tpu_custom_call" | custom-call | flops 30064771072 | bytes 22020096 | tf_op jit(solution)/shard_map/pallas_call | solution.py:489
  183.6 0.4 collective-permute-start
  184.0 0.0 copy-start
  184.0 8.6 %shard_map.112 = (bf16[512,3584]{1,0:T(8,128)(2,1)}, bf16[512,3584]{1,0:T(8,128)(2,1)}, bf16[512,3584]{1,0:T(8,128)(2,1)}) custom-call(bf16[512,3584]{1,0:T(8,128)(2,1)} %get-tuple-element.16.a_in, bf16[512,3584]{1,0:T(8,128)(2,1)} %get-tuple-element.17.b_in, bf16[512,3584]{1,0:T(8,128)(2,1)} %get-tuple-element.18.c_in), custom_call_target="tpu_custom_call" | custom-call | bytes 22020096 | tf_op jit(solution)/shard_map/pallas_call | solution.py:522
  192.6 0.0 collective-permute-done
  192.7 1.1 convert_add_fusion
  193.8 0.0 copy-done
  193.8 1.0 add_convert_fusion
Async XLA Ops:
  183.6 9.1 %collective-permute-start = (bf16[128,1024]{1,0:T(8,128)(2,1)}, bf16[128,1024]{1,0:T(8,128)(2,1)S(1)}, u32[]{:S(2)}, u32[]{:S(2)}) collective-permute-start(bf16[128,1024]{1,0:T(8,128)(2,1)} %get-tuple-element.15), channel_id=1, source_target_pairs={{0,2},{1,3},{2,0},{3,1},{4,6},{5,7},{6,4},{7,5},{8,10},{9,11},{10,... | collective-permute-start | bytes 786440 | tf_op jit(solution)/shard_map/ppermute | solution.py:521
  184.0 9.8 %copy-start = (bf16[128,2560]{1,0:T(8,128)(2,1)S(1)}, bf16[128,2560]{1,0:T(8,128)(2,1)}, u32[]{:S(2)}) copy-start(bf16[128,2560]{1,0:T(8,128)(2,1)} %get-tuple-element.13) | copy-start | bytes 1966084

commit v5 on v4

--- a/solution.py
+++ b/solution.py
@@ -24,8 +24,8 @@
 X_STEPS = sum(dx << (2 * q) for q, (dx, _) in enumerate(STEPS))
 Y_STEPS = sum(dy << (2 * q) for q, (_, dy) in enumerate(STEPS))
 WHOLE = ((0, D),)
-PIECES = ((0, 1536), (1536, 1024), (2560, 1024))
-LEAVE = 2560
+PIECES = ((0, 1024), (1024, 1024), (2048, 1536))
+LEAVE = 2048
 ENTRY = ((0, 1536), (1536, 2048))
 
 

time: 198 us -> 198 us (level)
  Pallas kernels: 192 us -> 187 us
  starting transfers between devices: 0.4 us -> 2.75 us
    pallas_call x1, Pallas kernels: 183 us -> 179 us  [per_device(): pl.pallas_call(kernel, out_shape=(jax.ShapeDtypeStruct((TOK, start), BF16...]
    ppermute x1, starting transfers between devices: 0.4 us -> 2.75 us  [per_device(): far = lax.ppermute(last, 'local', opposite)]
  transfers between devices with their start and end apart: 1 -> 1, of which waited for: 0 -> 1; matrix products, arithmetic and copies ran while one was open for 0% -> 0% of each run, Pallas kernels for 4% -> 4%
where the time goes in v5:
time: 198 us; the launch traced here: 195 us
  Pallas kernels  187 us (94%)
  other arithmetic  3.11 us (2%)
  starting transfers between devices  2.75 us (1%)
    pallas_call x1, Pallas kernels, per_device(): pl.pallas_call(kernel, out_shape=(jax.ShapeDtypeStruct((TOK, start), BF16...  179 us
    pallas_call x1, Pallas kernels, per_device(): pl.pallas_call(hand_over, out_shape=(grad, grad, grad), in_specs=[hbm] *...  8.65 us
  transfers between devices with their start and end apart: 1, of which 1 were waited for; matrix products, arithmetic and copies ran while one was open for 0% of the time, Pallas kernels for 4%

profile of v5, /device:TPU:26, one launch (start us, length us, event | category | flops | bytes accessed | tf_op | source)
XLA Modules:
  0.0 194.9 jit_solution(7175154938337384767)
XLA Ops:
  0.6 178.5 %shard_map.111 = (bf16[128,2048]{1,0:T(8,128)(2,1)}, bf16[128,1536]{1,0:T(8,128)(2,1)}, f32[128,1536]{1,0:T(8,128)}, bf16[512,3584]{1,0:T(8,128)(2,1)}, bf16[512...) custom-call(bf16[128,3584]{1,0:T(8,128)(2,1)} %tok.1, bf16[128,3584]{1,0:T(8,128)(2,1)} %cot.1, s32[2,128]{1,0:T(2,128)} %bitcast.3, ...), custom_call_target="tpu_custom_call" | custom-call | flops 30064771072 | bytes 22020096 | tf_op jit(solution)/shard_map/pallas_call | solution.py:489
  179.2 2.8 %collective-permute-start = (bf16[128,1536]{1,0:T(8,128)(2,1)}, bf16[128,1536]{1,0:T(8,128)(2,1)}, u32[]{:S(2)}, u32[]{:S(2)}) collective-permute-start(bf16[128,1536]{1,0:T(8,128)(2,1)} %get-tuple-element.15), channel_id=1, source_target_pairs={{0,2},{1,3},{2,0},{3,1},{4,6},{5,7},{6,4},{7,5},{8,10},{9,11},{10,... | collective-permute-start | bytes 1179656 | tf_op jit(solution)/shard_map/ppermute | solution.py:521
  181.9 0.0 copy-start
  181.9 8.7 %shard_map.112 = (bf16[512,3584]{1,0:T(8,128)(2,1)}, bf16[512,3584]{1,0:T(8,128)(2,1)}, bf16[512,3584]{1,0:T(8,128)(2,1)}) custom-call(bf16[512,3584]{1,0:T(8,128)(2,1)} %get-tuple-element.16.a_in, bf16[512,3584]{1,0:T(8,128)(2,1)} %get-tuple-element.17.b_in, bf16[512,3584]{1,0:T(8,128)(2,1)} %get-tuple-element.18.c_in), custom_call_target="tpu_custom_call" | custom-call | bytes 22020096 | tf_op jit(solution)/shard_map/pallas_call | solution.py:522
  190.6 1.2 collective-permute-done
  191.8 0.0 copy-done
  191.8 1.1 convert_add_fusion
  192.8 2.0 %add_convert_fusion = bf16[128,3584]{1,0:T(8,128)(2,1)} fusion(f32[128,1536]{1,0:T(8,128)S(1)} %convert_add_fusion, bf16[128,2048]{1,0:T(8,128)(2,1)} %get-tuple-element.13), kind=kLoop, calls=%fused_computation | loop fusion | flops 1376256 | bytes 2228224 | tf_op jit(solution)/shard_map/convert_element_type | solution.py:535
Async XLA Ops:
  179.2 12.6 %collective-permute-start = (bf16[128,1536]{1,0:T(8,128)(2,1)}, bf16[128,1536]{1,0:T(8,128)(2,1)}, u32[]{:S(2)}, u32[]{:S(2)}) collective-permute-start(bf16[128,1536]{1,0:T(8,128)(2,1)} %get-tuple-element.15), channel_id=1, source_target_pairs={{0,2},{1,3},{2,0},{3,1},{4,6},{5,7},{6,4},{7,5},{8,10},{9,11},{10,... | collective-permute-start | bytes 1179656 | tf_op jit(solution)/shard_map/ppermute | solution.py:521
  181.9 9.8 %copy-start = (f32[128,1536]{1,0:T(8,128)S(1)}, f32[128,1536]{1,0:T(8,128)}, u32[]{:S(2)}) copy-start(f32[128,1536]{1,0:T(8,128)} %get-tuple-element.14) | copy-start | bytes 2359300
